TPU v7x, 256 devices: a whole 4x4x8 slice. The times are simulated.
256 devices in a mesh: wide: 64 (over y, x, z_hi), narrow: 4 (over z_lo, core).
Axes of the slice: x: 4, y: 4, z: 8 (z_hi: 4, z_lo: 2; z = z_hi * 2 + z_lo), core: 2. Of those that a mesh axis runs over, the one named last changes fastest.
Arguments:
- gradient: bfloat16 [3072, 12800], P('wide', 'narrow'), may hold values from -1 to 1
Outputs:
- update: bfloat16 [3072, 12800], P('wide', 'narrow')
All inputs are finite; a program needn't handle non-finite values.
Results may differ from a plain program's by a relative error of at most 0.0059.
Values may be sent and summed in bfloat16 or wider, within the bound.
No kernel may reach another device: no remote copies, remote signals or barrier semaphores. Data moves between devices by JAX's collectives and lax.ppermute only.
A program may use at most 128 MiB of HBM per device.

v0:
```python
import functools
import math

import jax
import jax.numpy as jnp
import numpy as np
from jax import lax
from jax.experimental import pallas as pl
from jax.experimental.pallas import tpu as pltpu
from jax.sharding import Mesh, PartitionSpec as P

coef_a = 3.4445
coef_b = -4.775
coef_c = 2.0315

ALL = ("y", "x", "z", "zl", "core")
SIZES = (4, 4, 4, 2, 2)

STEP_MASKS = (4, 1, 12, 3)
Z_MASKS = ((1, 3), (3, 1))


def partners(function):
    pairs = []
    for i in range(math.prod(SIZES)):
        there = function(*(int(k) for k in np.unravel_index(i, SIZES)))
        pairs.append((i, int(np.ravel_multi_index(there, SIZES))))
    return pairs


def exchange(value, function):
    return lax.ppermute(value, ALL, partners(function))


def plane_mask(core, part, step):
    return STEP_MASKS[(step + 2 * core + part) % 4]


def swap_plane(value, part, step):
    def there(y, x, z, zl, core):
        mask = plane_mask(core, part, step)
        return y ^ (mask >> 2), x ^ (mask & 3), z, zl, core

    return exchange(value, there)


def swap_z(value, masks):
    return exchange(value, lambda y, x, z, zl, core: (y, x, z ^ masks[core], zl, core))


def swap_core(value):
    return exchange(value, lambda y, x, z, zl, core: (y, x, z, zl, core ^ 1))


def swap_zl(value):
    return exchange(value, lambda y, x, z, zl, core: (y, x, z, zl ^ 1, core))


def offsets(masks):
    found = [0]
    for mask in masks:
        found = found + [k ^ mask for k in found]
    return found


def multiply(a, b, dims):
    return lax.dot_general(a, b, (dims, ((), ())), preferred_element_type=jnp.float32)


def position():
    y, x, z, core = (lax.axis_index(k) for k in ("y", "x", "z", "core"))
    return y * 4 + x, z, core


def gathered_places(part):
    plane, _, core = position()
    orders = [offsets([plane_mask(c, part, step) for step in range(4)]) for c in range(2)]
    return [plane ^ jnp.where(core == 0, *pair) for pair in zip(*orders)]


def kept_half():
    _, z, core = position()
    return core ^ (z >> 1)


def gram_kernel(rows, c00, c01, c10, c11, near, far, *refs):
    keep, give, own, flip = refs
    _, z, core = position()
    orders = [offsets(masks) for masks in Z_MASKS]
    for k, pair in enumerate(zip(*orders)):
        at = pl.multiple_of((z ^ jnp.where(core == 0, *pair)) * rows, rows)
        ref = (near, far)[k // 2]
        own[pl.ds(at, rows), :] = ref[(k % 2) * rows : (k % 2 + 1) * rows, :]
    flip[:, 4 * rows :] = jnp.zeros((16 * rows, flip.shape[1] - 4 * rows), jnp.float32)
    start = 0
    for part, halves in enumerate(((c00, c01), (c10, c11))):
        width = halves[0].shape[1]
        places = gathered_places(part)
        for half in range(2):
            block = multiply(halves[half][...], own[:, start : start + width], ((1,), (1,)))
            for k in range(8):
                at = pl.multiple_of(places[8 * half + k] * rows, rows)
                value = block[k * rows : (k + 1) * rows, :]
                if part > 0:
                    value = value + flip[pl.ds(at, rows), 0 : 4 * rows]
                flip[pl.ds(at, rows), 0 : 4 * rows] = value
        start += width
    gram = flip[...].T
    first = kept_half() == 0
    keep[...] = jnp.where(first, gram[0 : 2 * rows], gram[2 * rows : 4 * rows])
    give[...] = jnp.where(first, gram[2 * rows : 4 * rows], gram[0 : 2 * rows])


def gram_halves(rows, pieces):
    vmem = pl.BlockSpec(memory_space=pltpu.VMEM)
    half = jax.ShapeDtypeStruct((2 * rows, 16 * rows), jnp.float32)
    padded = (4 * rows + 127) // 128 * 128
    return pl.pallas_call(
        functools.partial(gram_kernel, rows),
        out_shape=(half, half),
        in_specs=[vmem] * 6,
        out_specs=(vmem, vmem),
        scratch_shapes=[
            pltpu.VMEM((4 * rows, pieces[-1].shape[1]), jnp.bfloat16),
            pltpu.VMEM((16 * rows, padded), jnp.float32),
        ],
        compiler_params=pltpu.CompilerParams(vmem_limit_bytes=16 * 1024 * 1024),
    )(*pieces)


def mixer_kernel(rows, mine, other, *refs):
    outputs, (straight, flip, moved) = refs[:2], refs[2:]
    _, z, _ = position()
    for k in range(2):
        for half, ref in enumerate((mine, other)):
            at = pl.multiple_of(((2 * (kept_half() ^ half) + k) ^ z) * rows, rows)
            straight[pl.ds(at, rows), :] = ref[k * rows : (k + 1) * rows, :].astype(jnp.float32)
    straight[4 * rows :, :] = jnp.zeros((straight.shape[0] - 4 * rows, 16 * rows), jnp.float32)
    flip[...] = straight[...].T
    for part, ref in enumerate(outputs):
        for k, place in enumerate(gathered_places(part)):
            at = pl.multiple_of(place * rows, rows)
            moved[k * rows : (k + 1) * rows, :] = flip[pl.ds(at, rows), :]
        ref[...] = moved[...].T[0 : 4 * rows].astype(jnp.bfloat16)


def mixer_parts(rows, mine, other):
    vmem = pl.BlockSpec(memory_space=pltpu.VMEM)
    shape = jax.ShapeDtypeStruct((4 * rows, 16 * rows), jnp.bfloat16)
    padded = (4 * rows + 127) // 128 * 128
    return pl.pallas_call(
        functools.partial(mixer_kernel, rows),
        out_shape=(shape, shape),
        in_specs=[vmem] * 2,
        out_specs=(vmem, vmem),
        scratch_shapes=[
            pltpu.VMEM((padded, 16 * rows), jnp.float32),
            pltpu.VMEM((16 * rows, padded), jnp.float32),
            pltpu.VMEM((16 * rows, padded), jnp.float32),
        ],
        compiler_params=pltpu.CompilerParams(vmem_limit_bytes=8 * 1024 * 1024),
    )(mine, other)


def per_device(gradient):
    rows, cols = gradient.shape
    y, x, z = (lax.axis_index(k) for k in ("y", "x", "z"))
    zl, core = lax.axis_index("zl"), lax.axis_index("core")
    plane = y * 4 + x

    half = core ^ (z >> 1)
    choices = (half == 0, zl == (z & 1), core == 0, (z - 2 * half) * rows, plane * rows)
    gradient, choices = lax.optimization_barrier((gradient, choices))
    first_half, first_block, first_core, first_row, first_column = choices

    middle = cols // 2 // 128 * 128
    one_z = swap_z(gradient, (1, 3))
    one_z, other_z = lax.optimization_barrier((one_z, swap_z(gradient, (3, 1))))
    last_z = swap_z(one_z[:, :middle], (3, 1)), swap_z(other_z[:, middle:], (1, 3))
    far_z = [other_z, jnp.concatenate(last_z, 1)]
    parts = [gradient[:, :middle], gradient[:, middle:]]
    for step in range(3):
        parts = [
            jnp.concatenate([value, swap_plane(value, part, step)], 0)
            for part, value in enumerate(parts)
        ]
    pieces = []
    for part, value in enumerate(parts):
        pieces += [value, swap_plane(value, part, 3)]
    pieces += [jnp.concatenate([gradient, one_z], 0), jnp.concatenate(far_z, 0)]
    pieces = lax.optimization_barrier(pieces)

    width = 16 * rows

    row = lax.broadcasted_iota(jnp.int32, (2 * rows, width), 0) - first_row
    column = lax.broadcasted_iota(jnp.int32, (2 * rows, width), 1) - first_column
    diagonal = (row == column) & (row >= 0) & (row < rows)

    def add_zl(value):
        rounded = lax.reduce_precision(value, 8, 7)
        rest = jnp.sum(jnp.where(diagonal, value - rounded, 0.0), 0, keepdims=True)
        rest = jnp.broadcast_to(rest, (16, width))
        sent = jnp.concatenate([rounded, rest]).astype(jnp.bfloat16)
        got = swap_zl(sent).astype(jnp.float32)
        return value + got[: 2 * rows] + jnp.where(diagonal, got[2 * rows : 2 * rows + 1], 0.0)

    gram_half, given = gram_halves(rows, pieces)
    gram_half = add_zl(gram_half + swap_core(given)).astype(jnp.bfloat16)

    right = jnp.where(first_block, gram_half[:rows], gram_half[rows:])
    right = lax.all_to_all(
        jnp.broadcast_to(right[None], (16, rows, width)), ("y", "x"), 0, 0
    ).reshape(width, width)
    other = swap_core(gram_half)
    left = exchange(
        jnp.where(
            first_half, jnp.concatenate([gram_half, other]), jnp.concatenate([other, gram_half])
        ),
        lambda y, x, z, zl, core: (y, x, z ^ (2 * core + zl), zl, core),
    )
    square = jnp.dot(left, right, preferred_element_type=jnp.float32)
    halves = square[: 2 * rows], square[2 * rows :]
    square = jnp.where(first_half, halves[0], halves[1])
    square = add_zl(square + swap_core(jnp.where(first_half, halves[1], halves[0])))
    mixer = (coef_b * gram_half.astype(jnp.float32) + coef_c * square).astype(jnp.bfloat16)
    mixers = mixer_parts(rows, mixer, swap_core(mixer))

    sums = []
    for part, block in enumerate(mixers):
        product = jnp.dot(
            block[:, : 8 * rows], pieces[2 * part], preferred_element_type=jnp.float32
        ) + jnp.dot(
            block[:, 8 * rows :], pieces[2 * part + 1], preferred_element_type=jnp.float32
        )
        product = product.reshape(4, rows, product.shape[1])
        one, three = (1, 3) if part == 0 else (3, 1)
        near = jnp.where(first_core, product[one], product[three])
        far = jnp.where(first_core, product[three], product[one])
        moved = swap_z(product[2].astype(jnp.bfloat16), (three, one)).astype(jnp.float32)
        far = swap_z(far.astype(jnp.bfloat16), (three, one)).astype(jnp.float32)
        last = swap_z((near + moved).astype(jnp.bfloat16), (one, three))
        total = product[0] + far
        sums.append(total + last.astype(jnp.float32))
    combined = coef_a * gradient.astype(jnp.float32) + jnp.concatenate(sums, 1)
    factor = math.sqrt(float(cols * 4))
    return (combined * factor).astype(jnp.bfloat16)


def solution(mesh):
    split = Mesh(mesh.devices.reshape(SIZES), ALL)
    spec = P(("y", "x", "z"), ("zl", "core"))
    return jax.shard_map(
        per_device, mesh=split, in_specs=(spec,), out_specs=spec, check_vma=False
    )
```

profile of v0, /device:TPU:32, one launch (start us, length us, event | category | flops | bytes accessed | tf_op | source)
XLA Modules:
  0.0 126.6 jit_solution(11232314343937437716)
XLA Ops:
  0.0 0.9 slice.87
  0.9 1.6 %collective-permute-start.4 = (bf16[48,1664]{1,0:T(8,128)(2,1)S(1)}, bf16[48,1664]{1,0:T(8,128)(2,1)S(1)}, u32[]{:S(2)}, u32[]{:S(2)}) collective-permute-start(bf16[48,1664]{1,0:T(8,128)(2,1)S(1)} %slice.87), channel_id=1, source_target_pairs={{0,16},{1,49},{2,18},{3,51},{4,20},{5,53},{6,22},{7,55},{8,24},{9,... | collective-permute-start | bytes 479240 | tf_op jit(solution)/shard_map/ppermute | solution.py:32
  2.5 0.9 slice.86
  3.4 1.7 %collective-permute-start = (bf16[48,1536]{1,0:T(8,128)(2,1)S(1)}, bf16[48,1536]{1,0:T(8,128)(2,1)S(1)}, u32[]{:S(2)}, u32[]{:S(2)}) collective-permute-start(bf16[48,1536]{1,0:T(8,128)(2,1)S(1)} %slice.86), channel_id=1, source_target_pairs={{0,64},{1,193},{2,66},{3,195},{4,68},{5,197},{6,70},{7,199},{8,72}... | collective-permute-start | bytes 442376 | tf_op jit(solution)/shard_map/ppermute | solution.py:32
  5.1 1.2 collective-permute-done.4
  6.3 3.1 %collective-permute-start.5 = (bf16[96,1664]{1,0:T(8,128)(2,1)S(1)}, bf16[96,1664]{1,0:T(8,128)(2,1)S(1)}, u32[]{:S(2)}, u32[]{:S(2)}) collective-permute-start(bf16[96,1664]{1,0:T(8,128)(2,1)S(1)} %pad_maximum_fusion.5), channel_id=1, source_target_pairs={{0,192},{1,65},{2,194},{3,67},{4,196},{5,69},{6,198},{7,71},{8,200... | collective-permute-start | bytes 958472 | tf_op jit(solution)/shard_map/ppermute | solution.py:32
  9.5 1.6 %collective-permute-start.1 = (bf16[96,1536]{1,0:T(8,128)(2,1)S(1)}, bf16[96,1536]{1,0:T(8,128)(2,1)S(1)}, u32[]{:S(2)}, u32[]{:S(2)}) collective-permute-start(bf16[96,1536]{1,0:T(8,128)(2,1)S(1)} %pad_maximum_fusion.6), channel_id=1, source_target_pairs={{0,16},{1,49},{2,18},{3,51},{4,20},{5,53},{6,22},{7,55},{8,24},{9,... | collective-permute-start | bytes 884744 | tf_op jit(solution)/shard_map/ppermute | solution.py:32
  11.0 3.6 %collective-permute-done.5 = bf16[96,1664]{1,0:T(8,128)(2,1)S(1)} collective-permute-done((bf16[96,1664]{1,0:T(8,128)(2,1)S(1)}, bf16[96,1664]{1,0:T(8,128)(2,1)S(1)}, u32[]{:S(2)}, u32[]{:S(2)}) %collective-permute-start.5) | collective-permute-done | bytes 319520 | tf_op jit(solution)/shard_map/ppermute | solution.py:32
  14.6 0.1 pad_maximum_fusion.2
  14.7 2.8 %collective-permute-start.6 = (bf16[192,1664]{1,0:T(8,128)(2,1)S(1)}, bf16[192,1664]{1,0:T(8,128)(2,1)S(1)}, u32[]{:S(2)}, u32[]{:S(2)}) collective-permute-start(bf16[192,1664]{1,0:T(8,128)(2,1)S(1)} %pad_maximum_fusion.2), channel_id=1, source_target_pairs={{0,48},{1,17},{2,50},{3,19},{4,52},{5,21},{6,54},{7,23},{8,56},{9,... | collective-permute-start | bytes 1916936 | tf_op jit(solution)/shard_map/ppermute | solution.py:32
  17.6 3.1 %collective-permute-start.2 = (bf16[192,1536]{1,0:T(8,128)(2,1)S(1)}, bf16[192,1536]{1,0:T(8,128)(2,1)S(1)}, u32[]{:S(2)}, u32[]{:S(2)}) collective-permute-start(bf16[192,1536]{1,0:T(8,128)(2,1)S(1)} %pad_maximum_fusion.4), channel_id=1, source_target_pairs={{0,192},{1,65},{2,194},{3,67},{4,196},{5,69},{6,198},{7,71},{8,200... | collective-permute-start | bytes 1769480 | tf_op jit(solution)/shard_map/ppermute | solution.py:32
  20.7 3.3 %collective-permute-start.8 = (bf16[48,3200]{1,0:T(8,128)(2,1)S(1)}, bf16[48,3200]{1,0:T(8,128)(2,1)S(1)}, u32[]{:S(2)}, u32[]{:S(2)}) collective-permute-start(bf16[48,3200]{1,0:T(8,128)(2,1)S(1)} %copy-done.4), channel_id=1, source_target_pairs={{0,4},{1,13},{2,6},{3,15},{4,0},{5,9},{6,2},{7,11},{8,12},{9,5},{1... | collective-permute-start | bytes 921608 | tf_op jit(solution)/shard_map/ppermute | solution.py:32
  23.9 3.6 %collective-permute-start.9 = (bf16[48,3200]{1,0:T(8,128)(2,1)S(1)}, bf16[48,3200]{1,0:T(8,128)(2,1)S(1)}, u32[]{:S(2)}, u32[]{:S(2)}) collective-permute-start(bf16[48,3200]{1,0:T(8,128)(2,1)S(1)} %copy-done.4), channel_id=1, source_target_pairs={{0,12},{1,5},{2,14},{3,7},{4,8},{5,1},{6,10},{7,3},{8,4},{9,13},{1... | collective-permute-start | bytes 921608 | tf_op jit(solution)/shard_map/ppermute | solution.py:32
  27.5 0.1 pad_maximum_fusion.c10
  27.6 0.1 collective-permute-start.7
  27.7 2.4 %collective-permute-done.2 = bf16[192,1536]{1,0:T(8,128)(2,1)S(1)} collective-permute-done((bf16[192,1536]{1,0:T(8,128)(2,1)S(1)}, bf16[192,1536]{1,0:T(8,128)(2,1)S(1)}, u32[]{:S(2)}, u32[]{:S(2)}) %collective-permute-start.2) | collective-permute-done | bytes 589856 | tf_op jit(solution)/shard_map/ppermute | solution.py:32
  30.1 0.1 pad_maximum_fusion.1.c00
  30.2 2.5 %collective-permute-start.3 = (bf16[384,1536]{1,0:T(8,128)(2,1)S(1)}, bf16[384,1536]{1,0:T(8,128)(2,1)S(1)}, u32[]{:S(2)}, u32[]{:S(2)}) collective-permute-start(bf16[384,1536]{1,0:T(8,128)(2,1)S(1)} %pad_maximum_fusion.1.c00), channel_id=1, source_target_pairs={{0,48},{1,17},{2,50},{3,19},{4,52},{5,21},{6,54},{7,23},{8,56},{9,... | collective-permute-start | bytes 3538952 | tf_op jit(solution)/shard_map/ppermute | solution.py:32
  32.7 5.1 %collective-permute-done.8 = bf16[48,3200]{1,0:T(8,128)(2,1)S(1)} collective-permute-done((bf16[48,3200]{1,0:T(8,128)(2,1)S(1)}, bf16[48,3200]{1,0:T(8,128)(2,1)S(1)}, u32[]{:S(2)}, u32[]{:S(2)}) %collective-permute-start.8) | collective-permute-done | bytes 307232 | tf_op jit(solution)/shard_map/ppermute | solution.py:32
  37.8 2.5 %collective-permute-start.11 = (bf16[48,1664]{1,0:T(8,128)(2,1)S(1)}, bf16[48,1664]{1,0:T(8,128)(2,1)S(1)}, u32[]{:S(2)}, u32[]{:S(2)}) collective-permute-start(bf16[48,1664]{1,0:T(8,128)(2,1)S(1)} %slice.89), channel_id=1, source_target_pairs={{0,4},{1,13},{2,6},{3,15},{4,0},{5,9},{6,2},{7,11},{8,12},{9,5},{1... | collective-permute-start | bytes 479240 | tf_op jit(solution)/shard_map/ppermute | solution.py:32
  40.4 0.7 collective-permute-start.10
  41.1 7.7 %collective-permute-done.10 = bf16[48,1536]{1,0:T(8,128)(2,1)S(1)} collective-permute-done((bf16[48,1536]{1,0:T(8,128)(2,1)S(1)}, bf16[48,1536]{1,0:T(8,128)(2,1)S(1)}, u32[]{:S(2)}, u32[]{:S(2)}) %collective-permute-start.10) | collective-permute-done | bytes 147488 | tf_op jit(solution)/shard_map/ppermute | solution.py:32
  49.0 1.9 %shard_map.17 = (f32[96,768]{1,0:T(8,128)S(1)}, f32[96,768]{1,0:T(8,128)S(1)}) custom-call(bf16[384,1536]{1,0:T(8,128)(2,1)S(1)} %pad_maximum_fusion.1.c00, bf16[384,1536]{1,0:T(8,128)(2,1)S(1)} %collective-permute-done.3.c01, bf16[384,1664]{1,0:T(8,128)(2,1)S(1)} %pad_maximum_fusion.c10, bf16[384,1664]{1,0:T(8,128)(2,1)S(1)} %collective-permute-done.7.c11, ...), custom_call_target="tpu_custom_call" | custom-call | tf_op jit(solution)/shard_map/pallas_call | solution.py:118
  50.9 0.1 collective-permute-start.12
  51.1 1.5 %collective-permute-done.12 = f32[96,768]{1,0:T(8,128)S(1)} collective-permute-done((f32[96,768]{1,0:T(8,128)S(1)}, f32[96,768]{1,0:T(8,128)S(1)}, u32[]{:S(2)}, u32[]{:S(2)}) %collective-permute-start.12) | collective-permute-done | bytes 294944 | tf_op jit(solution)/shard_map/ppermute | solution.py:32
  52.6 0.2 fusion.4
  52.8 2.6 %collective-permute-start.13 = (bf16[112,768]{1,0:T(8,128)(2,1)S(1)}, bf16[112,768]{1,0:T(8,128)(2,1)S(1)}, u32[]{:S(2)}, u32[]{:S(2)}) collective-permute-start(bf16[112,768]{1,0:T(8,128)(2,1)S(1)} %pad_maximum_fusion.7), channel_id=1, source_target_pairs={{0,2},{1,3},{2,0},{3,1},{4,6},{5,7},{6,4},{7,5},{8,10},{9,11},{10,... | collective-permute-start | bytes 516104 | tf_op jit(solution)/shard_map/ppermute | solution.py:32
  55.4 4.7 %collective-permute-done.13 = bf16[112,768]{1,0:T(8,128)(2,1)S(1)} collective-permute-done((bf16[112,768]{1,0:T(8,128)(2,1)S(1)}, bf16[112,768]{1,0:T(8,128)(2,1)S(1)}, u32[]{:S(2)}, u32[]{:S(2)}) %collective-permute-start.13) | collective-permute-done | bytes 172064 | tf_op jit(solution)/shard_map/ppermute | solution.py:32
  60.2 0.1 fusion.13
  60.3 1.1 broadcast_in_dim.47
  61.4 4.4 %all-to-all-start = ((bf16[16,48,768]{2,1,0:T(8,128)(2,1)}), bf16[16,48,768]{2,1,0:T(8,128)(2,1)}, u32[]{:S(2)}, u32[]{:S(2)}) async-start(bf16[16,48,768]{2,1,0:T(8,128)(2,1)} %broadcast_in_dim.47), calls=%async_computation | async-start | bytes 2359296 | tf_op jit(solution)/shard_map/all_to_all | solution.py:211
  65.8 0.1 collective-permute-start.14
  65.9 1.4 %collective-permute-done.14 = bf16[96,768]{1,0:T(8,128)(2,1)S(1)} collective-permute-done((bf16[96,768]{1,0:T(8,128)(2,1)S(1)}, bf16[96,768]{1,0:T(8,128)(2,1)S(1)}, u32[]{:S(2)}, u32[]{:S(2)}) %collective-permute-start.14) | collective-permute-done | bytes 147488 | tf_op jit(solution)/shard_map/ppermute | solution.py:32
  67.3 0.1 maximum_select_fusion
  67.3 4.0 %collective-permute-start.15 = (bf16[192,768]{1,0:T(8,128)(2,1)S(1)}, bf16[192,768]{1,0:T(8,128)(2,1)S(1)}, u32[]{:S(2)}, u32[]{:S(2)}) collective-permute-start(bf16[192,768]{1,0:T(8,128)(2,1)S(1)} %maximum_select_fusion), channel_id=1, source_target_pairs={{0,0},{1,9},{2,6},{3,15},{4,4},{5,13},{6,2},{7,11},{8,8},{9,1},{10... | collective-permute-start | bytes 884744 | tf_op jit(solution)/shard_map/ppermute | solution.py:32
  71.4 7.8 %collective-permute-done.15 = bf16[192,768]{1,0:T(8,128)(2,1)S(1)} collective-permute-done((bf16[192,768]{1,0:T(8,128)(2,1)S(1)}, bf16[192,768]{1,0:T(8,128)(2,1)S(1)}, u32[]{:S(2)}, u32[]{:S(2)}) %collective-permute-start.15) | collective-permute-done | bytes 294944 | tf_op jit(solution)/shard_map/ppermute | solution.py:32
  79.1 6.0 %all-to-all-done = bf16[16,48,768]{2,1,0:T(8,128)(2,1)} async-done(((bf16[16,48,768]{2,1,0:T(8,128)(2,1)}), bf16[16,48,768]{2,1,0:T(8,128)(2,1)}, u32[]{:S(2)}, u32[]{:S(2)}) %all-to-all-start) | async-done | bytes 1179680 | tf_op jit(solution)/shard_map/all_to_all | solution.py:211
  85.1 1.7 %fusion.20 = f32[192,768]{1,0:T(8,128)S(1)} fusion(bf16[192,768]{1,0:T(8,128)(2,1)S(1)} %collective-permute-done.15, bf16[768,768]{1,0:T(8,128)(2,1)} %bitcast), kind=kOutput, calls=%fused_computation.58 | convolution fusion | flops 226492416 | bytes 2064384 | tf_op jit(solution)/shard_map/dot_general | solution.py:221
  86.9 0.3 collective-permute-start.16
  87.1 1.6 %collective-permute-done.16 = f32[96,768]{1,0:T(8,128)S(1)} collective-permute-done((f32[96,768]{1,0:T(8,128)S(1)}, f32[96,768]{1,0:T(8,128)S(1)}, u32[]{:S(2)}, u32[]{:S(2)}) %collective-permute-start.16) | collective-permute-done | bytes 294944 | tf_op jit(solution)/shard_map/ppermute | solution.py:32
  88.8 0.2 fusion.6
  89.0 1.5 %collective-permute-start.17 = (bf16[112,768]{1,0:T(8,128)(2,1)S(1)}, bf16[112,768]{1,0:T(8,128)(2,1)S(1)}, u32[]{:S(2)}, u32[]{:S(2)}) collective-permute-start(bf16[112,768]{1,0:T(8,128)(2,1)S(1)} %pad_maximum_fusion.8), channel_id=1, source_target_pairs={{0,2},{1,3},{2,0},{3,1},{4,6},{5,7},{6,4},{7,5},{8,10},{9,11},{10,... | collective-permute-start | bytes 516104 | tf_op jit(solution)/shard_map/ppermute | solution.py:32
  90.5 5.0 %collective-permute-done.17 = bf16[112,768]{1,0:T(8,128)(2,1)S(1)} collective-permute-done((bf16[112,768]{1,0:T(8,128)(2,1)S(1)}, bf16[112,768]{1,0:T(8,128)(2,1)S(1)}, u32[]{:S(2)}, u32[]{:S(2)}) %collective-permute-start.17) | collective-permute-done | bytes 172064 | tf_op jit(solution)/shard_map/ppermute | solution.py:32
  95.5 0.2 fusion.11.mine
  95.7 0.1 collective-permute-start.18
  95.8 1.4 %collective-permute-done.18.other = bf16[96,768]{1,0:T(8,128)(2,1)S(1)} collective-permute-done((bf16[96,768]{1,0:T(8,128)(2,1)S(1)}, bf16[96,768]{1,0:T(8,128)(2,1)S(1)}, u32[]{:S(2)}, u32[]{:S(2)}) %collective-permute-start.18) | collective-permute-done | bytes 147488 | tf_op jit(solution)/shard_map/ppermute | solution.py:32
  97.2 0.6 shard_map.18
  97.8 0.5 fusion.17
  98.3 0.5 convolution_add_fusion
  98.8 3.5 %collective-permute-start.20 = (bf16[48,1536]{1,0:T(8,128)(2,1)S(1)}, bf16[48,1536]{1,0:T(8,128)(2,1)S(1)}, u32[]{:S(2)}, u32[]{:S(2)}) collective-permute-start(bf16[48,1536]{1,0:T(8,128)(2,1)S(1)} %get-tuple-element.48), channel_id=1, source_target_pairs={{0,12},{1,5},{2,14},{3,7},{4,8},{5,1},{6,10},{7,3},{8,4},{9,13},{1... | collective-permute-start | bytes 442376 | tf_op jit(solution)/shard_map/ppermute | solution.py:32
  102.3 0.8 collective-permute-start.19
  103.0 0.5 fusion.14
  103.5 0.5 convolution_add_fusion.1
  104.0 0.1 select_convert_fusion
  104.1 1.3 %collective-permute-start.23 = (bf16[48,1664]{1,0:T(8,128)(2,1)S(1)}, bf16[48,1664]{1,0:T(8,128)(2,1)S(1)}, u32[]{:S(2)}, u32[]{:S(2)}) collective-permute-start(bf16[48,1664]{1,0:T(8,128)(2,1)S(1)} %get-tuple-element.46), channel_id=1, source_target_pairs={{0,4},{1,13},{2,6},{3,15},{4,0},{5,9},{6,2},{7,11},{8,12},{9,5},{1... | collective-permute-start | bytes 479240 | tf_op jit(solution)/shard_map/ppermute | solution.py:32
  105.4 1.7 %collective-permute-start.22 = (bf16[48,1664]{1,0:T(8,128)(2,1)S(1)}, bf16[48,1664]{1,0:T(8,128)(2,1)S(1)}, u32[]{:S(2)}, u32[]{:S(2)}) collective-permute-start(bf16[48,1664]{1,0:T(8,128)(2,1)S(1)} %get-tuple-element.45), channel_id=1, source_target_pairs={{0,4},{1,13},{2,6},{3,15},{4,0},{5,9},{6,2},{7,11},{8,12},{9,5},{1... | collective-permute-start | bytes 479240 | tf_op jit(solution)/shard_map/ppermute | solution.py:32
  107.1 0.8 collective-permute-done.20
  107.9 0.6 collective-permute-start.21
  108.5 7.4 %collective-permute-done.23 = bf16[48,1664]{1,0:T(8,128)(2,1)S(1)} collective-permute-done((bf16[48,1664]{1,0:T(8,128)(2,1)S(1)}, bf16[48,1664]{1,0:T(8,128)(2,1)S(1)}, u32[]{:S(2)}, u32[]{:S(2)}) %collective-permute-start.23) | collective-permute-done | bytes 159776 | tf_op jit(solution)/shard_map/ppermute | solution.py:32
  115.9 2.1 %collective-permute-start.24 = (bf16[48,1664]{1,0:T(8,128)(2,1)S(1)}, bf16[48,1664]{1,0:T(8,128)(2,1)S(1)}, u32[]{:S(2)}, u32[]{:S(2)}) collective-permute-start(bf16[48,1664]{1,0:T(8,128)(2,1)S(1)} %add_convert_fusion), channel_id=1, source_target_pairs={{0,12},{1,5},{2,14},{3,7},{4,8},{5,1},{6,10},{7,3},{8,4},{9,13},{1... | collective-permute-start | bytes 479240 | tf_op jit(solution)/shard_map/ppermute | solution.py:32
  118.0 1.8 %collective-permute-done.21 = bf16[48,1536]{1,0:T(8,128)(2,1)S(1)} collective-permute-done((bf16[48,1536]{1,0:T(8,128)(2,1)S(1)}, bf16[48,1536]{1,0:T(8,128)(2,1)S(1)}, u32[]{:S(2)}, u32[]{:S(2)}) %collective-permute-start.21) | collective-permute-done | bytes 147488 | tf_op jit(solution)/shard_map/ppermute | solution.py:32
  119.8 5.9 %collective-permute-done.24 = bf16[48,1664]{1,0:T(8,128)(2,1)S(1)} collective-permute-done((bf16[48,1664]{1,0:T(8,128)(2,1)S(1)}, bf16[48,1664]{1,0:T(8,128)(2,1)S(1)}, u32[]{:S(2)}, u32[]{:S(2)}) %collective-permute-start.24) | collective-permute-done | bytes 159776 | tf_op jit(solution)/shard_map/ppermute | solution.py:32
  125.7 0.1 fusion.2
  125.8 0.8 fusion.1
  (45 shorter events, 0.7 us)
Async XLA Ops:
  0.9 5.4 %collective-permute-start.4 = (bf16[48,1664]{1,0:T(8,128)(2,1)S(1)}, bf16[48,1664]{1,0:T(8,128)(2,1)S(1)}, u32[]{:S(2)}, u32[]{:S(2)}) collective-permute-start(bf16[48,1664]{1,0:T(8,128)(2,1)S(1)} %slice.87), channel_id=1, source_target_pairs={{0,16},{1,49},{2,18},{3,51},{4,20},{5,53},{6,22},{7,55},{8,24},{9,... | collective-permute-start | bytes 479240 | tf_op jit(solution)/shard_map/ppermute | solution.py:32
  3.4 6.0 %collective-permute-start = (bf16[48,1536]{1,0:T(8,128)(2,1)S(1)}, bf16[48,1536]{1,0:T(8,128)(2,1)S(1)}, u32[]{:S(2)}, u32[]{:S(2)}) collective-permute-start(bf16[48,1536]{1,0:T(8,128)(2,1)S(1)} %slice.86), channel_id=1, source_target_pairs={{0,64},{1,193},{2,66},{3,195},{4,68},{5,197},{6,70},{7,199},{8,72}... | collective-permute-start | bytes 442376 | tf_op jit(solution)/shard_map/ppermute | solution.py:32
  6.3 8.3 %collective-permute-start.5 = (bf16[96,1664]{1,0:T(8,128)(2,1)S(1)}, bf16[96,1664]{1,0:T(8,128)(2,1)S(1)}, u32[]{:S(2)}, u32[]{:S(2)}) collective-permute-start(bf16[96,1664]{1,0:T(8,128)(2,1)S(1)} %pad_maximum_fusion.5), channel_id=1, source_target_pairs={{0,192},{1,65},{2,194},{3,67},{4,196},{5,69},{6,198},{7,71},{8,200... | collective-permute-start | bytes 958472 | tf_op jit(solution)/shard_map/ppermute | solution.py:32
  9.5 11.2 %copy-start.4 = (bf16[48,3200]{1,0:T(8,128)(2,1)S(1)}, bf16[48,3200]{1,0:T(8,128)(2,1)}, u32[]{:S(2)}) copy-start(bf16[48,3200]{1,0:T(8,128)(2,1)} %param.1) | copy-start | bytes 921604
  9.5 8.0 %collective-permute-start.1 = (bf16[96,1536]{1,0:T(8,128)(2,1)S(1)}, bf16[96,1536]{1,0:T(8,128)(2,1)S(1)}, u32[]{:S(2)}, u32[]{:S(2)}) collective-permute-start(bf16[96,1536]{1,0:T(8,128)(2,1)S(1)} %pad_maximum_fusion.6), channel_id=1, source_target_pairs={{0,16},{1,49},{2,18},{3,51},{4,20},{5,53},{6,22},{7,55},{8,24},{9,... | collective-permute-start | bytes 884744 | tf_op jit(solution)/shard_map/ppermute | solution.py:32
  14.7 12.9 %collective-permute-start.6 = (bf16[192,1664]{1,0:T(8,128)(2,1)S(1)}, bf16[192,1664]{1,0:T(8,128)(2,1)S(1)}, u32[]{:S(2)}, u32[]{:S(2)}) collective-permute-start(bf16[192,1664]{1,0:T(8,128)(2,1)S(1)} %pad_maximum_fusion.2), channel_id=1, source_target_pairs={{0,48},{1,17},{2,50},{3,19},{4,52},{5,21},{6,54},{7,23},{8,56},{9,... | collective-permute-start | bytes 1916936 | tf_op jit(solution)/shard_map/ppermute | solution.py:32
  17.6 12.6 %collective-permute-start.2 = (bf16[192,1536]{1,0:T(8,128)(2,1)S(1)}, bf16[192,1536]{1,0:T(8,128)(2,1)S(1)}, u32[]{:S(2)}, u32[]{:S(2)}) collective-permute-start(bf16[192,1536]{1,0:T(8,128)(2,1)S(1)} %pad_maximum_fusion.4), channel_id=1, source_target_pairs={{0,192},{1,65},{2,194},{3,67},{4,196},{5,69},{6,198},{7,71},{8,200... | collective-permute-start | bytes 1769480 | tf_op jit(solution)/shard_map/ppermute | solution.py:32
  20.7 17.1 %collective-permute-start.8 = (bf16[48,3200]{1,0:T(8,128)(2,1)S(1)}, bf16[48,3200]{1,0:T(8,128)(2,1)S(1)}, u32[]{:S(2)}, u32[]{:S(2)}) collective-permute-start(bf16[48,3200]{1,0:T(8,128)(2,1)S(1)} %copy-done.4), channel_id=1, source_target_pairs={{0,4},{1,13},{2,6},{3,15},{4,0},{5,9},{6,2},{7,11},{8,12},{9,5},{1... | collective-permute-start | bytes 921608 | tf_op jit(solution)/shard_map/ppermute | solution.py:32
  23.9 13.9 %collective-permute-start.9 = (bf16[48,3200]{1,0:T(8,128)(2,1)S(1)}, bf16[48,3200]{1,0:T(8,128)(2,1)S(1)}, u32[]{:S(2)}, u32[]{:S(2)}) collective-permute-start(bf16[48,3200]{1,0:T(8,128)(2,1)S(1)} %copy-done.4), channel_id=1, source_target_pairs={{0,12},{1,5},{2,14},{3,7},{4,8},{5,1},{6,10},{7,3},{8,4},{9,13},{1... | collective-permute-start | bytes 921608 | tf_op jit(solution)/shard_map/ppermute | solution.py:32
  27.6 21.3 %collective-permute-start.7 = (bf16[384,1664]{1,0:T(8,128)(2,1)S(1)}, bf16[384,1664]{1,0:T(8,128)(2,1)S(1)}, u32[]{:S(2)}, u32[]{:S(2)}) collective-permute-start(bf16[384,1664]{1,0:T(8,128)(2,1)S(1)} %pad_maximum_fusion.c10), channel_id=1, source_target_pairs={{0,64},{1,193},{2,66},{3,195},{4,68},{5,197},{6,70},{7,199},{8,72}... | collective-permute-start | bytes 3833864 | tf_op jit(solution)/shard_map/ppermute | solution.py:32
  30.2 18.7 %collective-permute-start.3 = (bf16[384,1536]{1,0:T(8,128)(2,1)S(1)}, bf16[384,1536]{1,0:T(8,128)(2,1)S(1)}, u32[]{:S(2)}, u32[]{:S(2)}) collective-permute-start(bf16[384,1536]{1,0:T(8,128)(2,1)S(1)} %pad_maximum_fusion.1.c00), channel_id=1, source_target_pairs={{0,48},{1,17},{2,50},{3,19},{4,52},{5,21},{6,54},{7,23},{8,56},{9,... | collective-permute-start | bytes 3538952 | tf_op jit(solution)/shard_map/ppermute | solution.py:32
  37.8 11.1 %collective-permute-start.11 = (bf16[48,1664]{1,0:T(8,128)(2,1)S(1)}, bf16[48,1664]{1,0:T(8,128)(2,1)S(1)}, u32[]{:S(2)}, u32[]{:S(2)}) collective-permute-start(bf16[48,1664]{1,0:T(8,128)(2,1)S(1)} %slice.89), channel_id=1, source_target_pairs={{0,4},{1,13},{2,6},{3,15},{4,0},{5,9},{6,2},{7,11},{8,12},{9,5},{1... | collective-permute-start | bytes 479240 | tf_op jit(solution)/shard_map/ppermute | solution.py:32
  40.4 8.5 %collective-permute-start.10 = (bf16[48,1536]{1,0:T(8,128)(2,1)S(1)}, bf16[48,1536]{1,0:T(8,128)(2,1)S(1)}, u32[]{:S(2)}, u32[]{:S(2)}) collective-permute-start(bf16[48,1536]{1,0:T(8,128)(2,1)S(1)} %slice.88), channel_id=1, source_target_pairs={{0,12},{1,5},{2,14},{3,7},{4,8},{5,1},{6,10},{7,3},{8,4},{9,13},{1... | collective-permute-start | bytes 442376 | tf_op jit(solution)/shard_map/ppermute | solution.py:32
  48.9 2.0 %copy-start.2 = (bf16[384,1536]{1,0:T(8,128)(2,1)}, bf16[384,1536]{1,0:T(8,128)(2,1)S(1)}, u32[]{:S(2)}) copy-start(bf16[384,1536]{1,0:T(8,128)(2,1)S(1)} %collective-permute-done.3.c01) | copy-start | bytes 3538948
  49.0 2.0 %copy-start = (bf16[384,1664]{1,0:T(8,128)(2,1)}, bf16[384,1664]{1,0:T(8,128)(2,1)S(1)}, u32[]{:S(2)}) copy-start(bf16[384,1664]{1,0:T(8,128)(2,1)S(1)} %collective-permute-done.7.c11) | copy-start | bytes 3833860
  50.9 1.7 %collective-permute-start.12 = (f32[96,768]{1,0:T(8,128)S(1)}, f32[96,768]{1,0:T(8,128)S(1)}, u32[]{:S(2)}, u32[]{:S(2)}) collective-permute-start(f32[96,768]{1,0:T(8,128)S(1)} %get-tuple-element.33), channel_id=1, source_target_pairs={{0,1},{1,0},{2,3},{3,2},{4,5},{5,4},{6,7},{7,6},{8,9},{9,8},{10,11... | collective-permute-start | bytes 884744 | tf_op jit(solution)/shard_map/ppermute | solution.py:32
  52.8 7.3 %collective-permute-start.13 = (bf16[112,768]{1,0:T(8,128)(2,1)S(1)}, bf16[112,768]{1,0:T(8,128)(2,1)S(1)}, u32[]{:S(2)}, u32[]{:S(2)}) collective-permute-start(bf16[112,768]{1,0:T(8,128)(2,1)S(1)} %pad_maximum_fusion.7), channel_id=1, source_target_pairs={{0,2},{1,3},{2,0},{3,1},{4,6},{5,7},{6,4},{7,5},{8,10},{9,11},{10,... | collective-permute-start | bytes 516104 | tf_op jit(solution)/shard_map/ppermute | solution.py:32
  61.4 23.7 %all-to-all-start = ((bf16[16,48,768]{2,1,0:T(8,128)(2,1)}), bf16[16,48,768]{2,1,0:T(8,128)(2,1)}, u32[]{:S(2)}, u32[]{:S(2)}) async-start(bf16[16,48,768]{2,1,0:T(8,128)(2,1)} %broadcast_in_dim.47), calls=%async_computation | async-start | bytes 2359296 | tf_op jit(solution)/shard_map/all_to_all | solution.py:211
  65.8 1.5 %collective-permute-start.14 = (bf16[96,768]{1,0:T(8,128)(2,1)S(1)}, bf16[96,768]{1,0:T(8,128)(2,1)S(1)}, u32[]{:S(2)}, u32[]{:S(2)}) collective-permute-start(bf16[96,768]{1,0:T(8,128)(2,1)S(1)} %fusion.13), channel_id=1, source_target_pairs={{0,1},{1,0},{2,3},{3,2},{4,5},{5,4},{6,7},{7,6},{8,9},{9,8},{10,11... | collective-permute-start | bytes 442376 | tf_op jit(solution)/shard_map/ppermute | solution.py:32
  67.3 11.8 %collective-permute-start.15 = (bf16[192,768]{1,0:T(8,128)(2,1)S(1)}, bf16[192,768]{1,0:T(8,128)(2,1)S(1)}, u32[]{:S(2)}, u32[]{:S(2)}) collective-permute-start(bf16[192,768]{1,0:T(8,128)(2,1)S(1)} %maximum_select_fusion), channel_id=1, source_target_pairs={{0,0},{1,9},{2,6},{3,15},{4,4},{5,13},{6,2},{7,11},{8,8},{9,1},{10... | collective-permute-start | bytes 884744 | tf_op jit(solution)/shard_map/ppermute | solution.py:32
  86.9 1.9 %collective-permute-start.16 = (f32[96,768]{1,0:T(8,128)S(1)}, f32[96,768]{1,0:T(8,128)S(1)}, u32[]{:S(2)}, u32[]{:S(2)}) collective-permute-start(f32[96,768]{1,0:T(8,128)S(1)} %slice_select_fusion), channel_id=1, source_target_pairs={{0,1},{1,0},{2,3},{3,2},{4,5},{5,4},{6,7},{7,6},{8,9},{9,8},{10,11... | collective-permute-start | bytes 884744 | tf_op jit(solution)/shard_map/ppermute | solution.py:32
  88.8 9.0 %copy-start.3 = (bf16[384,1536]{1,0:T(8,128)(2,1)S(1)}, bf16[384,1536]{1,0:T(8,128)(2,1)}, u32[]{:S(2)}) copy-start(bf16[384,1536]{1,0:T(8,128)(2,1)} %copy-done.2) | copy-start | bytes 3538948
  89.0 6.5 %collective-permute-start.17 = (bf16[112,768]{1,0:T(8,128)(2,1)S(1)}, bf16[112,768]{1,0:T(8,128)(2,1)S(1)}, u32[]{:S(2)}, u32[]{:S(2)}) collective-permute-start(bf16[112,768]{1,0:T(8,128)(2,1)S(1)} %pad_maximum_fusion.8), channel_id=1, source_target_pairs={{0,2},{1,3},{2,0},{3,1},{4,6},{5,7},{6,4},{7,5},{8,10},{9,11},{10,... | collective-permute-start | bytes 516104 | tf_op jit(solution)/shard_map/ppermute | solution.py:32
  95.7 1.5 %collective-permute-start.18 = (bf16[96,768]{1,0:T(8,128)(2,1)S(1)}, bf16[96,768]{1,0:T(8,128)(2,1)S(1)}, u32[]{:S(2)}, u32[]{:S(2)}) collective-permute-start(bf16[96,768]{1,0:T(8,128)(2,1)S(1)} %fusion.11.mine), channel_id=1, source_target_pairs={{0,1},{1,0},{2,3},{3,2},{4,5},{5,4},{6,7},{7,6},{8,9},{9,8},{10,11... | collective-permute-start | bytes 442376 | tf_op jit(solution)/shard_map/ppermute | solution.py:32
  98.2 4.8 %copy-start.1 = (bf16[384,1664]{1,0:T(8,128)(2,1)S(1)}, bf16[384,1664]{1,0:T(8,128)(2,1)}, u32[]{:S(2)}) copy-start(bf16[384,1664]{1,0:T(8,128)(2,1)} %copy-done) | copy-start | bytes 3833860
  98.8 9.1 %collective-permute-start.20 = (bf16[48,1536]{1,0:T(8,128)(2,1)S(1)}, bf16[48,1536]{1,0:T(8,128)(2,1)S(1)}, u32[]{:S(2)}, u32[]{:S(2)}) collective-permute-start(bf16[48,1536]{1,0:T(8,128)(2,1)S(1)} %get-tuple-element.48), channel_id=1, source_target_pairs={{0,12},{1,5},{2,14},{3,7},{4,8},{5,1},{6,10},{7,3},{8,4},{9,13},{1... | collective-permute-start | bytes 442376 | tf_op jit(solution)/shard_map/ppermute | solution.py:32
  102.3 15.8 %collective-permute-start.19 = (bf16[48,1536]{1,0:T(8,128)(2,1)S(1)}, bf16[48,1536]{1,0:T(8,128)(2,1)S(1)}, u32[]{:S(2)}, u32[]{:S(2)}) collective-permute-start(bf16[48,1536]{1,0:T(8,128)(2,1)S(1)} %get-tuple-element.47), channel_id=1, source_target_pairs={{0,12},{1,5},{2,14},{3,7},{4,8},{5,1},{6,10},{7,3},{8,4},{9,13},{1... | collective-permute-start | bytes 442376 | tf_op jit(solution)/shard_map/ppermute | solution.py:32
  104.1 11.8 %collective-permute-start.23 = (bf16[48,1664]{1,0:T(8,128)(2,1)S(1)}, bf16[48,1664]{1,0:T(8,128)(2,1)S(1)}, u32[]{:S(2)}, u32[]{:S(2)}) collective-permute-start(bf16[48,1664]{1,0:T(8,128)(2,1)S(1)} %get-tuple-element.46), channel_id=1, source_target_pairs={{0,4},{1,13},{2,6},{3,15},{4,0},{5,9},{6,2},{7,11},{8,12},{9,5},{1... | collective-permute-start | bytes 479240 | tf_op jit(solution)/shard_map/ppermute | solution.py:32
  105.4 14.4 %collective-permute-start.22 = (bf16[48,1664]{1,0:T(8,128)(2,1)S(1)}, bf16[48,1664]{1,0:T(8,128)(2,1)S(1)}, u32[]{:S(2)}, u32[]{:S(2)}) collective-permute-start(bf16[48,1664]{1,0:T(8,128)(2,1)S(1)} %get-tuple-element.45), channel_id=1, source_target_pairs={{0,4},{1,13},{2,6},{3,15},{4,0},{5,9},{6,2},{7,11},{8,12},{9,5},{1... | collective-permute-start | bytes 479240 | tf_op jit(solution)/shard_map/ppermute | solution.py:32
  107.9 11.9 %collective-permute-start.21 = (bf16[48,1536]{1,0:T(8,128)(2,1)S(1)}, bf16[48,1536]{1,0:T(8,128)(2,1)S(1)}, u32[]{:S(2)}, u32[]{:S(2)}) collective-permute-start(bf16[48,1536]{1,0:T(8,128)(2,1)S(1)} %add_convert_fusion.1), channel_id=1, source_target_pairs={{0,4},{1,13},{2,6},{3,15},{4,0},{5,9},{6,2},{7,11},{8,12},{9,5},{1... | collective-permute-start | bytes 442376 | tf_op jit(solution)/shard_map/ppermute | solution.py:32
  115.9 9.8 %collective-permute-start.24 = (bf16[48,1664]{1,0:T(8,128)(2,1)S(1)}, bf16[48,1664]{1,0:T(8,128)(2,1)S(1)}, u32[]{:S(2)}, u32[]{:S(2)}) collective-permute-start(bf16[48,1664]{1,0:T(8,128)(2,1)S(1)} %add_convert_fusion), channel_id=1, source_target_pairs={{0,12},{1,5},{2,14},{3,7},{4,8},{5,1},{6,10},{7,3},{8,4},{9,13},{1... | collective-permute-start | bytes 479240 | tf_op jit(solution)/shard_map/ppermute | solution.py:32
where the time goes:
time: 127 us
  waiting for transfers between devices  65.1 us (51%)
  starting transfers between devices  49.5 us (39%)
  matrix products  3.63 us (3%)
  local copies, waits for them, and re-layouts  3.02 us (2%)
  Pallas kernels  2.52 us (2%)
  other arithmetic  2.43 us (2%)
    ppermute x25, waiting for transfers between devices, exchange(): return lax.ppermute(value, ALL, partners(function))  59.1 us
    ppermute x25, starting transfers between devices, exchange(): return lax.ppermute(value, ALL, partners(function))  45.1 us
    all_to_all x1, waiting for transfers between devices, per_device(): lax.all_to_all(jnp.broadcast_to(right[None], (16, rows, width)), ('y', 'x...  6 us
    all_to_all x1, starting transfers between devices, per_device(): lax.all_to_all(jnp.broadcast_to(right[None], (16, rows, width)), ('y', 'x...  4.38 us
  transfers between devices with their start and end apart: 26, of which 17 were waited for; matrix products, arithmetic and copies ran while one was open for 2% of the time, Pallas kernels for 0%

commit v1 on v0

--- a/solution.py
+++ b/solution.py
@@ -226,7 +226,7 @@
     mixers = mixer_parts(rows, mixer, swap_core(mixer))
 
     sums = []
-    for part, block in enumerate(mixers):
+    for part, block in reversed(list(enumerate(mixers))):
         product = jnp.dot(
             block[:, : 8 * rows], pieces[2 * part], preferred_element_type=jnp.float32
         ) + jnp.dot(
@@ -241,7 +241,7 @@
         last = swap_z((near + moved).astype(jnp.bfloat16), (one, three))
         total = product[0] + far
         sums.append(total + last.astype(jnp.float32))
-    combined = coef_a * gradient.astype(jnp.float32) + jnp.concatenate(sums, 1)
+    combined = coef_a * gradient.astype(jnp.float32) + jnp.concatenate(sums[::-1], 1)
     factor = math.sqrt(float(cols * 4))
     return (combined * factor).astype(jnp.bfloat16)
 

time: 127 us -> 127 us (level)
  no operation moved by 1% of the time
where the time goes in v1:
time: 127 us
  waiting for transfers between devices  65.1 us (51%)
  starting transfers between devices  49.5 us (39%)
  matrix products  3.63 us (3%)
  local copies, waits for them, and re-layouts  3.02 us (2%)
  Pallas kernels  2.52 us (2%)
  other arithmetic  2.43 us (2%)
    ppermute x25, waiting for transfers between devices, exchange(): return lax.ppermute(value, ALL, partners(function))  59.1 us
    ppermute x25, starting transfers between devices, exchange(): return lax.ppermute(value, ALL, partners(function))  45.1 us
    all_to_all x1, waiting for transfers between devices, per_device(): lax.all_to_all(jnp.broadcast_to(right[None], (16, rows, width)), ('y', 'x...  6 us
    all_to_all x1, starting transfers between devices, per_device(): lax.all_to_all(jnp.broadcast_to(right[None], (16, rows, width)), ('y', 'x...  4.38 us
  transfers between devices with their start and end apart: 26, of which 17 were waited for; matrix products, arithmetic and copies ran while one was open for 2% of the time, Pallas kernels for 0%

profile of v1, /device:TPU:32, one launch (start us, length us, event | category | flops | bytes accessed | tf_op | source)
XLA Modules:
  0.0 126.6 jit_solution(11232314343937437716)
XLA Ops:
  0.0 0.9 slice.87
  0.9 1.6 %collective-permute-start.4 = (bf16[48,1664]{1,0:T(8,128)(2,1)S(1)}, bf16[48,1664]{1,0:T(8,128)(2,1)S(1)}, u32[]{:S(2)}, u32[]{:S(2)}) collective-permute-start(bf16[48,1664]{1,0:T(8,128)(2,1)S(1)} %slice.87), channel_id=1, source_target_pairs={{0,16},{1,49},{2,18},{3,51},{4,20},{5,53},{6,22},{7,55},{8,24},{9,... | collective-permute-start | bytes 479240 | tf_op jit(solution)/shard_map/ppermute | solution.py:32
  2.5 0.9 slice.86
  3.4 1.7 %collective-permute-start = (bf16[48,1536]{1,0:T(8,128)(2,1)S(1)}, bf16[48,1536]{1,0:T(8,128)(2,1)S(1)}, u32[]{:S(2)}, u32[]{:S(2)}) collective-permute-start(bf16[48,1536]{1,0:T(8,128)(2,1)S(1)} %slice.86), channel_id=1, source_target_pairs={{0,64},{1,193},{2,66},{3,195},{4,68},{5,197},{6,70},{7,199},{8,72}... | collective-permute-start | bytes 442376 | tf_op jit(solution)/shard_map/ppermute | solution.py:32
  5.1 1.2 collective-permute-done.4
  6.3 3.1 %collective-permute-start.5 = (bf16[96,1664]{1,0:T(8,128)(2,1)S(1)}, bf16[96,1664]{1,0:T(8,128)(2,1)S(1)}, u32[]{:S(2)}, u32[]{:S(2)}) collective-permute-start(bf16[96,1664]{1,0:T(8,128)(2,1)S(1)} %pad_maximum_fusion.5), channel_id=1, source_target_pairs={{0,192},{1,65},{2,194},{3,67},{4,196},{5,69},{6,198},{7,71},{8,200... | collective-permute-start | bytes 958472 | tf_op jit(solution)/shard_map/ppermute | solution.py:32
  9.5 1.6 %collective-permute-start.1 = (bf16[96,1536]{1,0:T(8,128)(2,1)S(1)}, bf16[96,1536]{1,0:T(8,128)(2,1)S(1)}, u32[]{:S(2)}, u32[]{:S(2)}) collective-permute-start(bf16[96,1536]{1,0:T(8,128)(2,1)S(1)} %pad_maximum_fusion.6), channel_id=1, source_target_pairs={{0,16},{1,49},{2,18},{3,51},{4,20},{5,53},{6,22},{7,55},{8,24},{9,... | collective-permute-start | bytes 884744 | tf_op jit(solution)/shard_map/ppermute | solution.py:32
  11.0 3.6 %collective-permute-done.5 = bf16[96,1664]{1,0:T(8,128)(2,1)S(1)} collective-permute-done((bf16[96,1664]{1,0:T(8,128)(2,1)S(1)}, bf16[96,1664]{1,0:T(8,128)(2,1)S(1)}, u32[]{:S(2)}, u32[]{:S(2)}) %collective-permute-start.5) | collective-permute-done | bytes 319520 | tf_op jit(solution)/shard_map/ppermute | solution.py:32
  14.6 0.1 pad_maximum_fusion.2
  14.7 2.8 %collective-permute-start.6 = (bf16[192,1664]{1,0:T(8,128)(2,1)S(1)}, bf16[192,1664]{1,0:T(8,128)(2,1)S(1)}, u32[]{:S(2)}, u32[]{:S(2)}) collective-permute-start(bf16[192,1664]{1,0:T(8,128)(2,1)S(1)} %pad_maximum_fusion.2), channel_id=1, source_target_pairs={{0,48},{1,17},{2,50},{3,19},{4,52},{5,21},{6,54},{7,23},{8,56},{9,... | collective-permute-start | bytes 1916936 | tf_op jit(solution)/shard_map/ppermute | solution.py:32
  17.6 3.1 %collective-permute-start.2 = (bf16[192,1536]{1,0:T(8,128)(2,1)S(1)}, bf16[192,1536]{1,0:T(8,128)(2,1)S(1)}, u32[]{:S(2)}, u32[]{:S(2)}) collective-permute-start(bf16[192,1536]{1,0:T(8,128)(2,1)S(1)} %pad_maximum_fusion.4), channel_id=1, source_target_pairs={{0,192},{1,65},{2,194},{3,67},{4,196},{5,69},{6,198},{7,71},{8,200... | collective-permute-start | bytes 1769480 | tf_op jit(solution)/shard_map/ppermute | solution.py:32
  20.7 3.3 %collective-permute-start.8 = (bf16[48,3200]{1,0:T(8,128)(2,1)S(1)}, bf16[48,3200]{1,0:T(8,128)(2,1)S(1)}, u32[]{:S(2)}, u32[]{:S(2)}) collective-permute-start(bf16[48,3200]{1,0:T(8,128)(2,1)S(1)} %copy-done.4), channel_id=1, source_target_pairs={{0,4},{1,13},{2,6},{3,15},{4,0},{5,9},{6,2},{7,11},{8,12},{9,5},{1... | collective-permute-start | bytes 921608 | tf_op jit(solution)/shard_map/ppermute | solution.py:32
  23.9 3.6 %collective-permute-start.9 = (bf16[48,3200]{1,0:T(8,128)(2,1)S(1)}, bf16[48,3200]{1,0:T(8,128)(2,1)S(1)}, u32[]{:S(2)}, u32[]{:S(2)}) collective-permute-start(bf16[48,3200]{1,0:T(8,128)(2,1)S(1)} %copy-done.4), channel_id=1, source_target_pairs={{0,12},{1,5},{2,14},{3,7},{4,8},{5,1},{6,10},{7,3},{8,4},{9,13},{1... | collective-permute-start | bytes 921608 | tf_op jit(solution)/shard_map/ppermute | solution.py:32
  27.5 0.1 pad_maximum_fusion.c10
  27.6 0.1 collective-permute-start.7
  27.7 2.4 %collective-permute-done.2 = bf16[192,1536]{1,0:T(8,128)(2,1)S(1)} collective-permute-done((bf16[192,1536]{1,0:T(8,128)(2,1)S(1)}, bf16[192,1536]{1,0:T(8,128)(2,1)S(1)}, u32[]{:S(2)}, u32[]{:S(2)}) %collective-permute-start.2) | collective-permute-done | bytes 589856 | tf_op jit(solution)/shard_map/ppermute | solution.py:32
  30.1 0.1 pad_maximum_fusion.1.c00
  30.2 2.5 %collective-permute-start.3 = (bf16[384,1536]{1,0:T(8,128)(2,1)S(1)}, bf16[384,1536]{1,0:T(8,128)(2,1)S(1)}, u32[]{:S(2)}, u32[]{:S(2)}) collective-permute-start(bf16[384,1536]{1,0:T(8,128)(2,1)S(1)} %pad_maximum_fusion.1.c00), channel_id=1, source_target_pairs={{0,48},{1,17},{2,50},{3,19},{4,52},{5,21},{6,54},{7,23},{8,56},{9,... | collective-permute-start | bytes 3538952 | tf_op jit(solution)/shard_map/ppermute | solution.py:32
  32.7 5.1 %collective-permute-done.8 = bf16[48,3200]{1,0:T(8,128)(2,1)S(1)} collective-permute-done((bf16[48,3200]{1,0:T(8,128)(2,1)S(1)}, bf16[48,3200]{1,0:T(8,128)(2,1)S(1)}, u32[]{:S(2)}, u32[]{:S(2)}) %collective-permute-start.8) | collective-permute-done | bytes 307232 | tf_op jit(solution)/shard_map/ppermute | solution.py:32
  37.8 2.5 %collective-permute-start.11 = (bf16[48,1664]{1,0:T(8,128)(2,1)S(1)}, bf16[48,1664]{1,0:T(8,128)(2,1)S(1)}, u32[]{:S(2)}, u32[]{:S(2)}) collective-permute-start(bf16[48,1664]{1,0:T(8,128)(2,1)S(1)} %slice.89), channel_id=1, source_target_pairs={{0,4},{1,13},{2,6},{3,15},{4,0},{5,9},{6,2},{7,11},{8,12},{9,5},{1... | collective-permute-start | bytes 479240 | tf_op jit(solution)/shard_map/ppermute | solution.py:32
  40.4 0.7 collective-permute-start.10
  41.1 7.7 %collective-permute-done.10 = bf16[48,1536]{1,0:T(8,128)(2,1)S(1)} collective-permute-done((bf16[48,1536]{1,0:T(8,128)(2,1)S(1)}, bf16[48,1536]{1,0:T(8,128)(2,1)S(1)}, u32[]{:S(2)}, u32[]{:S(2)}) %collective-permute-start.10) | collective-permute-done | bytes 147488 | tf_op jit(solution)/shard_map/ppermute | solution.py:32
  49.0 1.9 %shard_map.17 = (f32[96,768]{1,0:T(8,128)S(1)}, f32[96,768]{1,0:T(8,128)S(1)}) custom-call(bf16[384,1536]{1,0:T(8,128)(2,1)S(1)} %pad_maximum_fusion.1.c00, bf16[384,1536]{1,0:T(8,128)(2,1)S(1)} %collective-permute-done.3.c01, bf16[384,1664]{1,0:T(8,128)(2,1)S(1)} %pad_maximum_fusion.c10, bf16[384,1664]{1,0:T(8,128)(2,1)S(1)} %collective-permute-done.7.c11, ...), custom_call_target="tpu_custom_call" | custom-call | tf_op jit(solution)/shard_map/pallas_call | solution.py:118
  50.9 0.1 collective-permute-start.12
  51.1 1.5 %collective-permute-done.12 = f32[96,768]{1,0:T(8,128)S(1)} collective-permute-done((f32[96,768]{1,0:T(8,128)S(1)}, f32[96,768]{1,0:T(8,128)S(1)}, u32[]{:S(2)}, u32[]{:S(2)}) %collective-permute-start.12) | collective-permute-done | bytes 294944 | tf_op jit(solution)/shard_map/ppermute | solution.py:32
  52.6 0.2 fusion.4
  52.8 2.6 %collective-permute-start.13 = (bf16[112,768]{1,0:T(8,128)(2,1)S(1)}, bf16[112,768]{1,0:T(8,128)(2,1)S(1)}, u32[]{:S(2)}, u32[]{:S(2)}) collective-permute-start(bf16[112,768]{1,0:T(8,128)(2,1)S(1)} %pad_maximum_fusion.7), channel_id=1, source_target_pairs={{0,2},{1,3},{2,0},{3,1},{4,6},{5,7},{6,4},{7,5},{8,10},{9,11},{10,... | collective-permute-start | bytes 516104 | tf_op jit(solution)/shard_map/ppermute | solution.py:32
  55.4 4.7 %collective-permute-done.13 = bf16[112,768]{1,0:T(8,128)(2,1)S(1)} collective-permute-done((bf16[112,768]{1,0:T(8,128)(2,1)S(1)}, bf16[112,768]{1,0:T(8,128)(2,1)S(1)}, u32[]{:S(2)}, u32[]{:S(2)}) %collective-permute-start.13) | collective-permute-done | bytes 172064 | tf_op jit(solution)/shard_map/ppermute | solution.py:32
  60.2 0.1 fusion.13
  60.3 1.1 broadcast_in_dim.47
  61.4 4.4 %all-to-all-start = ((bf16[16,48,768]{2,1,0:T(8,128)(2,1)}), bf16[16,48,768]{2,1,0:T(8,128)(2,1)}, u32[]{:S(2)}, u32[]{:S(2)}) async-start(bf16[16,48,768]{2,1,0:T(8,128)(2,1)} %broadcast_in_dim.47), calls=%async_computation | async-start | bytes 2359296 | tf_op jit(solution)/shard_map/all_to_all | solution.py:211
  65.8 0.1 collective-permute-start.14
  65.9 1.4 %collective-permute-done.14 = bf16[96,768]{1,0:T(8,128)(2,1)S(1)} collective-permute-done((bf16[96,768]{1,0:T(8,128)(2,1)S(1)}, bf16[96,768]{1,0:T(8,128)(2,1)S(1)}, u32[]{:S(2)}, u32[]{:S(2)}) %collective-permute-start.14) | collective-permute-done | bytes 147488 | tf_op jit(solution)/shard_map/ppermute | solution.py:32
  67.3 0.1 maximum_select_fusion
  67.3 4.0 %collective-permute-start.15 = (bf16[192,768]{1,0:T(8,128)(2,1)S(1)}, bf16[192,768]{1,0:T(8,128)(2,1)S(1)}, u32[]{:S(2)}, u32[]{:S(2)}) collective-permute-start(bf16[192,768]{1,0:T(8,128)(2,1)S(1)} %maximum_select_fusion), channel_id=1, source_target_pairs={{0,0},{1,9},{2,6},{3,15},{4,4},{5,13},{6,2},{7,11},{8,8},{9,1},{10... | collective-permute-start | bytes 884744 | tf_op jit(solution)/shard_map/ppermute | solution.py:32
  71.4 7.8 %collective-permute-done.15 = bf16[192,768]{1,0:T(8,128)(2,1)S(1)} collective-permute-done((bf16[192,768]{1,0:T(8,128)(2,1)S(1)}, bf16[192,768]{1,0:T(8,128)(2,1)S(1)}, u32[]{:S(2)}, u32[]{:S(2)}) %collective-permute-start.15) | collective-permute-done | bytes 294944 | tf_op jit(solution)/shard_map/ppermute | solution.py:32
  79.1 6.0 %all-to-all-done = bf16[16,48,768]{2,1,0:T(8,128)(2,1)} async-done(((bf16[16,48,768]{2,1,0:T(8,128)(2,1)}), bf16[16,48,768]{2,1,0:T(8,128)(2,1)}, u32[]{:S(2)}, u32[]{:S(2)}) %all-to-all-start) | async-done | bytes 1179680 | tf_op jit(solution)/shard_map/all_to_all | solution.py:211
  85.1 1.7 %fusion.20 = f32[192,768]{1,0:T(8,128)S(1)} fusion(bf16[192,768]{1,0:T(8,128)(2,1)S(1)} %collective-permute-done.15, bf16[768,768]{1,0:T(8,128)(2,1)} %bitcast), kind=kOutput, calls=%fused_computation.58 | convolution fusion | flops 226492416 | bytes 2064384 | tf_op jit(solution)/shard_map/dot_general | solution.py:221
  86.9 0.3 collective-permute-start.16
  87.1 1.6 %collective-permute-done.16 = f32[96,768]{1,0:T(8,128)S(1)} collective-permute-done((f32[96,768]{1,0:T(8,128)S(1)}, f32[96,768]{1,0:T(8,128)S(1)}, u32[]{:S(2)}, u32[]{:S(2)}) %collective-permute-start.16) | collective-permute-done | bytes 294944 | tf_op jit(solution)/shard_map/ppermute | solution.py:32
  88.8 0.2 fusion.6
  89.0 1.5 %collective-permute-start.17 = (bf16[112,768]{1,0:T(8,128)(2,1)S(1)}, bf16[112,768]{1,0:T(8,128)(2,1)S(1)}, u32[]{:S(2)}, u32[]{:S(2)}) collective-permute-start(bf16[112,768]{1,0:T(8,128)(2,1)S(1)} %pad_maximum_fusion.8), channel_id=1, source_target_pairs={{0,2},{1,3},{2,0},{3,1},{4,6},{5,7},{6,4},{7,5},{8,10},{9,11},{10,... | collective-permute-start | bytes 516104 | tf_op jit(solution)/shard_map/ppermute | solution.py:32
  90.5 5.0 %collective-permute-done.17 = bf16[112,768]{1,0:T(8,128)(2,1)S(1)} collective-permute-done((bf16[112,768]{1,0:T(8,128)(2,1)S(1)}, bf16[112,768]{1,0:T(8,128)(2,1)S(1)}, u32[]{:S(2)}, u32[]{:S(2)}) %collective-permute-start.17) | collective-permute-done | bytes 172064 | tf_op jit(solution)/shard_map/ppermute | solution.py:32
  95.5 0.2 fusion.11.mine
  95.7 0.1 collective-permute-start.18
  95.8 1.4 %collective-permute-done.18.other = bf16[96,768]{1,0:T(8,128)(2,1)S(1)} collective-permute-done((bf16[96,768]{1,0:T(8,128)(2,1)S(1)}, bf16[96,768]{1,0:T(8,128)(2,1)S(1)}, u32[]{:S(2)}, u32[]{:S(2)}) %collective-permute-start.18) | collective-permute-done | bytes 147488 | tf_op jit(solution)/shard_map/ppermute | solution.py:32
  97.2 0.6 shard_map.18
  97.8 0.5 fusion.17
  98.3 0.5 convolution_add_fusion
  98.8 3.5 %collective-permute-start.20 = (bf16[48,1536]{1,0:T(8,128)(2,1)S(1)}, bf16[48,1536]{1,0:T(8,128)(2,1)S(1)}, u32[]{:S(2)}, u32[]{:S(2)}) collective-permute-start(bf16[48,1536]{1,0:T(8,128)(2,1)S(1)} %get-tuple-element.48), channel_id=1, source_target_pairs={{0,12},{1,5},{2,14},{3,7},{4,8},{5,1},{6,10},{7,3},{8,4},{9,13},{1... | collective-permute-start | bytes 442376 | tf_op jit(solution)/shard_map/ppermute | solution.py:32
  102.3 0.8 collective-permute-start.19
  103.0 0.5 fusion.14
  103.5 0.5 convolution_add_fusion.1
  104.0 0.1 select_convert_fusion
  104.1 1.3 %collective-permute-start.23 = (bf16[48,1664]{1,0:T(8,128)(2,1)S(1)}, bf16[48,1664]{1,0:T(8,128)(2,1)S(1)}, u32[]{:S(2)}, u32[]{:S(2)}) collective-permute-start(bf16[48,1664]{1,0:T(8,128)(2,1)S(1)} %get-tuple-element.46), channel_id=1, source_target_pairs={{0,4},{1,13},{2,6},{3,15},{4,0},{5,9},{6,2},{7,11},{8,12},{9,5},{1... | collective-permute-start | bytes 479240 | tf_op jit(solution)/shard_map/ppermute | solution.py:32
  105.4 1.7 %collective-permute-start.22 = (bf16[48,1664]{1,0:T(8,128)(2,1)S(1)}, bf16[48,1664]{1,0:T(8,128)(2,1)S(1)}, u32[]{:S(2)}, u32[]{:S(2)}) collective-permute-start(bf16[48,1664]{1,0:T(8,128)(2,1)S(1)} %get-tuple-element.45), channel_id=1, source_target_pairs={{0,4},{1,13},{2,6},{3,15},{4,0},{5,9},{6,2},{7,11},{8,12},{9,5},{1... | collective-permute-start | bytes 479240 | tf_op jit(solution)/shard_map/ppermute | solution.py:32
  107.1 0.8 collective-permute-done.20
  107.9 0.6 collective-permute-start.21
  108.5 7.4 %collective-permute-done.23 = bf16[48,1664]{1,0:T(8,128)(2,1)S(1)} collective-permute-done((bf16[48,1664]{1,0:T(8,128)(2,1)S(1)}, bf16[48,1664]{1,0:T(8,128)(2,1)S(1)}, u32[]{:S(2)}, u32[]{:S(2)}) %collective-permute-start.23) | collective-permute-done | bytes 159776 | tf_op jit(solution)/shard_map/ppermute | solution.py:32
  115.9 2.1 %collective-permute-start.24 = (bf16[48,1664]{1,0:T(8,128)(2,1)S(1)}, bf16[48,1664]{1,0:T(8,128)(2,1)S(1)}, u32[]{:S(2)}, u32[]{:S(2)}) collective-permute-start(bf16[48,1664]{1,0:T(8,128)(2,1)S(1)} %add_convert_fusion), channel_id=1, source_target_pairs={{0,12},{1,5},{2,14},{3,7},{4,8},{5,1},{6,10},{7,3},{8,4},{9,13},{1... | collective-permute-start | bytes 479240 | tf_op jit(solution)/shard_map/ppermute | solution.py:32
  118.0 1.8 %collective-permute-done.21 = bf16[48,1536]{1,0:T(8,128)(2,1)S(1)} collective-permute-done((bf16[48,1536]{1,0:T(8,128)(2,1)S(1)}, bf16[48,1536]{1,0:T(8,128)(2,1)S(1)}, u32[]{:S(2)}, u32[]{:S(2)}) %collective-permute-start.21) | collective-permute-done | bytes 147488 | tf_op jit(solution)/shard_map/ppermute | solution.py:32
  119.8 5.9 %collective-permute-done.24 = bf16[48,1664]{1,0:T(8,128)(2,1)S(1)} collective-permute-done((bf16[48,1664]{1,0:T(8,128)(2,1)S(1)}, bf16[48,1664]{1,0:T(8,128)(2,1)S(1)}, u32[]{:S(2)}, u32[]{:S(2)}) %collective-permute-start.24) | collective-permute-done | bytes 159776 | tf_op jit(solution)/shard_map/ppermute | solution.py:32
  125.7 0.1 fusion.2
  125.8 0.8 fusion.1
  (45 shorter events, 0.7 us)
Async XLA Ops:
  0.9 5.4 %collective-permute-start.4 = (bf16[48,1664]{1,0:T(8,128)(2,1)S(1)}, bf16[48,1664]{1,0:T(8,128)(2,1)S(1)}, u32[]{:S(2)}, u32[]{:S(2)}) collective-permute-start(bf16[48,1664]{1,0:T(8,128)(2,1)S(1)} %slice.87), channel_id=1, source_target_pairs={{0,16},{1,49},{2,18},{3,51},{4,20},{5,53},{6,22},{7,55},{8,24},{9,... | collective-permute-start | bytes 479240 | tf_op jit(solution)/shard_map/ppermute | solution.py:32
  3.4 6.0 %collective-permute-start = (bf16[48,1536]{1,0:T(8,128)(2,1)S(1)}, bf16[48,1536]{1,0:T(8,128)(2,1)S(1)}, u32[]{:S(2)}, u32[]{:S(2)}) collective-permute-start(bf16[48,1536]{1,0:T(8,128)(2,1)S(1)} %slice.86), channel_id=1, source_target_pairs={{0,64},{1,193},{2,66},{3,195},{4,68},{5,197},{6,70},{7,199},{8,72}... | collective-permute-start | bytes 442376 | tf_op jit(solution)/shard_map/ppermute | solution.py:32
  6.3 8.3 %collective-permute-start.5 = (bf16[96,1664]{1,0:T(8,128)(2,1)S(1)}, bf16[96,1664]{1,0:T(8,128)(2,1)S(1)}, u32[]{:S(2)}, u32[]{:S(2)}) collective-permute-start(bf16[96,1664]{1,0:T(8,128)(2,1)S(1)} %pad_maximum_fusion.5), channel_id=1, source_target_pairs={{0,192},{1,65},{2,194},{3,67},{4,196},{5,69},{6,198},{7,71},{8,200... | collective-permute-start | bytes 958472 | tf_op jit(solution)/shard_map/ppermute | solution.py:32
  9.5 11.2 %copy-start.4 = (bf16[48,3200]{1,0:T(8,128)(2,1)S(1)}, bf16[48,3200]{1,0:T(8,128)(2,1)}, u32[]{:S(2)}) copy-start(bf16[48,3200]{1,0:T(8,128)(2,1)} %param.1) | copy-start | bytes 921604
  9.5 8.0 %collective-permute-start.1 = (bf16[96,1536]{1,0:T(8,128)(2,1)S(1)}, bf16[96,1536]{1,0:T(8,128)(2,1)S(1)}, u32[]{:S(2)}, u32[]{:S(2)}) collective-permute-start(bf16[96,1536]{1,0:T(8,128)(2,1)S(1)} %pad_maximum_fusion.6), channel_id=1, source_target_pairs={{0,16},{1,49},{2,18},{3,51},{4,20},{5,53},{6,22},{7,55},{8,24},{9,... | collective-permute-start | bytes 884744 | tf_op jit(solution)/shard_map/ppermute | solution.py:32
  14.7 12.9 %collective-permute-start.6 = (bf16[192,1664]{1,0:T(8,128)(2,1)S(1)}, bf16[192,1664]{1,0:T(8,128)(2,1)S(1)}, u32[]{:S(2)}, u32[]{:S(2)}) collective-permute-start(bf16[192,1664]{1,0:T(8,128)(2,1)S(1)} %pad_maximum_fusion.2), channel_id=1, source_target_pairs={{0,48},{1,17},{2,50},{3,19},{4,52},{5,21},{6,54},{7,23},{8,56},{9,... | collective-permute-start | bytes 1916936 | tf_op jit(solution)/shard_map/ppermute | solution.py:32
  17.6 12.6 %collective-permute-start.2 = (bf16[192,1536]{1,0:T(8,128)(2,1)S(1)}, bf16[192,1536]{1,0:T(8,128)(2,1)S(1)}, u32[]{:S(2)}, u32[]{:S(2)}) collective-permute-start(bf16[192,1536]{1,0:T(8,128)(2,1)S(1)} %pad_maximum_fusion.4), channel_id=1, source_target_pairs={{0,192},{1,65},{2,194},{3,67},{4,196},{5,69},{6,198},{7,71},{8,200... | collective-permute-start | bytes 1769480 | tf_op jit(solution)/shard_map/ppermute | solution.py:32
  20.7 17.1 %collective-permute-start.8 = (bf16[48,3200]{1,0:T(8,128)(2,1)S(1)}, bf16[48,3200]{1,0:T(8,128)(2,1)S(1)}, u32[]{:S(2)}, u32[]{:S(2)}) collective-permute-start(bf16[48,3200]{1,0:T(8,128)(2,1)S(1)} %copy-done.4), channel_id=1, source_target_pairs={{0,4},{1,13},{2,6},{3,15},{4,0},{5,9},{6,2},{7,11},{8,12},{9,5},{1... | collective-permute-start | bytes 921608 | tf_op jit(solution)/shard_map/ppermute | solution.py:32
  23.9 13.9 %collective-permute-start.9 = (bf16[48,3200]{1,0:T(8,128)(2,1)S(1)}, bf16[48,3200]{1,0:T(8,128)(2,1)S(1)}, u32[]{:S(2)}, u32[]{:S(2)}) collective-permute-start(bf16[48,3200]{1,0:T(8,128)(2,1)S(1)} %copy-done.4), channel_id=1, source_target_pairs={{0,12},{1,5},{2,14},{3,7},{4,8},{5,1},{6,10},{7,3},{8,4},{9,13},{1... | collective-permute-start | bytes 921608 | tf_op jit(solution)/shard_map/ppermute | solution.py:32
  27.6 21.3 %collective-permute-start.7 = (bf16[384,1664]{1,0:T(8,128)(2,1)S(1)}, bf16[384,1664]{1,0:T(8,128)(2,1)S(1)}, u32[]{:S(2)}, u32[]{:S(2)}) collective-permute-start(bf16[384,1664]{1,0:T(8,128)(2,1)S(1)} %pad_maximum_fusion.c10), channel_id=1, source_target_pairs={{0,64},{1,193},{2,66},{3,195},{4,68},{5,197},{6,70},{7,199},{8,72}... | collective-permute-start | bytes 3833864 | tf_op jit(solution)/shard_map/ppermute | solution.py:32
  30.2 18.7 %collective-permute-start.3 = (bf16[384,1536]{1,0:T(8,128)(2,1)S(1)}, bf16[384,1536]{1,0:T(8,128)(2,1)S(1)}, u32[]{:S(2)}, u32[]{:S(2)}) collective-permute-start(bf16[384,1536]{1,0:T(8,128)(2,1)S(1)} %pad_maximum_fusion.1.c00), channel_id=1, source_target_pairs={{0,48},{1,17},{2,50},{3,19},{4,52},{5,21},{6,54},{7,23},{8,56},{9,... | collective-permute-start | bytes 3538952 | tf_op jit(solution)/shard_map/ppermute | solution.py:32
  37.8 11.1 %collective-permute-start.11 = (bf16[48,1664]{1,0:T(8,128)(2,1)S(1)}, bf16[48,1664]{1,0:T(8,128)(2,1)S(1)}, u32[]{:S(2)}, u32[]{:S(2)}) collective-permute-start(bf16[48,1664]{1,0:T(8,128)(2,1)S(1)} %slice.89), channel_id=1, source_target_pairs={{0,4},{1,13},{2,6},{3,15},{4,0},{5,9},{6,2},{7,11},{8,12},{9,5},{1... | collective-permute-start | bytes 479240 | tf_op jit(solution)/shard_map/ppermute | solution.py:32
  40.4 8.5 %collective-permute-start.10 = (bf16[48,1536]{1,0:T(8,128)(2,1)S(1)}, bf16[48,1536]{1,0:T(8,128)(2,1)S(1)}, u32[]{:S(2)}, u32[]{:S(2)}) collective-permute-start(bf16[48,1536]{1,0:T(8,128)(2,1)S(1)} %slice.88), channel_id=1, source_target_pairs={{0,12},{1,5},{2,14},{3,7},{4,8},{5,1},{6,10},{7,3},{8,4},{9,13},{1... | collective-permute-start | bytes 442376 | tf_op jit(solution)/shard_map/ppermute | solution.py:32
  48.9 2.0 %copy-start.2 = (bf16[384,1536]{1,0:T(8,128)(2,1)}, bf16[384,1536]{1,0:T(8,128)(2,1)S(1)}, u32[]{:S(2)}) copy-start(bf16[384,1536]{1,0:T(8,128)(2,1)S(1)} %collective-permute-done.3.c01) | copy-start | bytes 3538948
  49.0 2.0 %copy-start = (bf16[384,1664]{1,0:T(8,128)(2,1)}, bf16[384,1664]{1,0:T(8,128)(2,1)S(1)}, u32[]{:S(2)}) copy-start(bf16[384,1664]{1,0:T(8,128)(2,1)S(1)} %collective-permute-done.7.c11) | copy-start | bytes 3833860
  50.9 1.7 %collective-permute-start.12 = (f32[96,768]{1,0:T(8,128)S(1)}, f32[96,768]{1,0:T(8,128)S(1)}, u32[]{:S(2)}, u32[]{:S(2)}) collective-permute-start(f32[96,768]{1,0:T(8,128)S(1)} %get-tuple-element.33), channel_id=1, source_target_pairs={{0,1},{1,0},{2,3},{3,2},{4,5},{5,4},{6,7},{7,6},{8,9},{9,8},{10,11... | collective-permute-start | bytes 884744 | tf_op jit(solution)/shard_map/ppermute | solution.py:32
  52.8 7.3 %collective-permute-start.13 = (bf16[112,768]{1,0:T(8,128)(2,1)S(1)}, bf16[112,768]{1,0:T(8,128)(2,1)S(1)}, u32[]{:S(2)}, u32[]{:S(2)}) collective-permute-start(bf16[112,768]{1,0:T(8,128)(2,1)S(1)} %pad_maximum_fusion.7), channel_id=1, source_target_pairs={{0,2},{1,3},{2,0},{3,1},{4,6},{5,7},{6,4},{7,5},{8,10},{9,11},{10,... | collective-permute-start | bytes 516104 | tf_op jit(solution)/shard_map/ppermute | solution.py:32
  61.4 23.7 %all-to-all-start = ((bf16[16,48,768]{2,1,0:T(8,128)(2,1)}), bf16[16,48,768]{2,1,0:T(8,128)(2,1)}, u32[]{:S(2)}, u32[]{:S(2)}) async-start(bf16[16,48,768]{2,1,0:T(8,128)(2,1)} %broadcast_in_dim.47), calls=%async_computation | async-start | bytes 2359296 | tf_op jit(solution)/shard_map/all_to_all | solution.py:211
  65.8 1.5 %collective-permute-start.14 = (bf16[96,768]{1,0:T(8,128)(2,1)S(1)}, bf16[96,768]{1,0:T(8,128)(2,1)S(1)}, u32[]{:S(2)}, u32[]{:S(2)}) collective-permute-start(bf16[96,768]{1,0:T(8,128)(2,1)S(1)} %fusion.13), channel_id=1, source_target_pairs={{0,1},{1,0},{2,3},{3,2},{4,5},{5,4},{6,7},{7,6},{8,9},{9,8},{10,11... | collective-permute-start | bytes 442376 | tf_op jit(solution)/shard_map/ppermute | solution.py:32
  67.3 11.8 %collective-permute-start.15 = (bf16[192,768]{1,0:T(8,128)(2,1)S(1)}, bf16[192,768]{1,0:T(8,128)(2,1)S(1)}, u32[]{:S(2)}, u32[]{:S(2)}) collective-permute-start(bf16[192,768]{1,0:T(8,128)(2,1)S(1)} %maximum_select_fusion), channel_id=1, source_target_pairs={{0,0},{1,9},{2,6},{3,15},{4,4},{5,13},{6,2},{7,11},{8,8},{9,1},{10... | collective-permute-start | bytes 884744 | tf_op jit(solution)/shard_map/ppermute | solution.py:32
  86.9 1.9 %collective-permute-start.16 = (f32[96,768]{1,0:T(8,128)S(1)}, f32[96,768]{1,0:T(8,128)S(1)}, u32[]{:S(2)}, u32[]{:S(2)}) collective-permute-start(f32[96,768]{1,0:T(8,128)S(1)} %slice_select_fusion), channel_id=1, source_target_pairs={{0,1},{1,0},{2,3},{3,2},{4,5},{5,4},{6,7},{7,6},{8,9},{9,8},{10,11... | collective-permute-start | bytes 884744 | tf_op jit(solution)/shard_map/ppermute | solution.py:32
  88.8 9.0 %copy-start.3 = (bf16[384,1536]{1,0:T(8,128)(2,1)S(1)}, bf16[384,1536]{1,0:T(8,128)(2,1)}, u32[]{:S(2)}) copy-start(bf16[384,1536]{1,0:T(8,128)(2,1)} %copy-done.2) | copy-start | bytes 3538948
  89.0 6.5 %collective-permute-start.17 = (bf16[112,768]{1,0:T(8,128)(2,1)S(1)}, bf16[112,768]{1,0:T(8,128)(2,1)S(1)}, u32[]{:S(2)}, u32[]{:S(2)}) collective-permute-start(bf16[112,768]{1,0:T(8,128)(2,1)S(1)} %pad_maximum_fusion.8), channel_id=1, source_target_pairs={{0,2},{1,3},{2,0},{3,1},{4,6},{5,7},{6,4},{7,5},{8,10},{9,11},{10,... | collective-permute-start | bytes 516104 | tf_op jit(solution)/shard_map/ppermute | solution.py:32
  95.7 1.5 %collective-permute-start.18 = (bf16[96,768]{1,0:T(8,128)(2,1)S(1)}, bf16[96,768]{1,0:T(8,128)(2,1)S(1)}, u32[]{:S(2)}, u32[]{:S(2)}) collective-permute-start(bf16[96,768]{1,0:T(8,128)(2,1)S(1)} %fusion.11.mine), channel_id=1, source_target_pairs={{0,1},{1,0},{2,3},{3,2},{4,5},{5,4},{6,7},{7,6},{8,9},{9,8},{10,11... | collective-permute-start | bytes 442376 | tf_op jit(solution)/shard_map/ppermute | solution.py:32
  98.2 4.8 %copy-start.1 = (bf16[384,1664]{1,0:T(8,128)(2,1)S(1)}, bf16[384,1664]{1,0:T(8,128)(2,1)}, u32[]{:S(2)}) copy-start(bf16[384,1664]{1,0:T(8,128)(2,1)} %copy-done) | copy-start | bytes 3833860
  98.8 9.1 %collective-permute-start.20 = (bf16[48,1536]{1,0:T(8,128)(2,1)S(1)}, bf16[48,1536]{1,0:T(8,128)(2,1)S(1)}, u32[]{:S(2)}, u32[]{:S(2)}) collective-permute-start(bf16[48,1536]{1,0:T(8,128)(2,1)S(1)} %get-tuple-element.48), channel_id=1, source_target_pairs={{0,12},{1,5},{2,14},{3,7},{4,8},{5,1},{6,10},{7,3},{8,4},{9,13},{1... | collective-permute-start | bytes 442376 | tf_op jit(solution)/shard_map/ppermute | solution.py:32
  102.3 15.8 %collective-permute-start.19 = (bf16[48,1536]{1,0:T(8,128)(2,1)S(1)}, bf16[48,1536]{1,0:T(8,128)(2,1)S(1)}, u32[]{:S(2)}, u32[]{:S(2)}) collective-permute-start(bf16[48,1536]{1,0:T(8,128)(2,1)S(1)} %get-tuple-element.47), channel_id=1, source_target_pairs={{0,12},{1,5},{2,14},{3,7},{4,8},{5,1},{6,10},{7,3},{8,4},{9,13},{1... | collective-permute-start | bytes 442376 | tf_op jit(solution)/shard_map/ppermute | solution.py:32
  104.1 11.8 %collective-permute-start.23 = (bf16[48,1664]{1,0:T(8,128)(2,1)S(1)}, bf16[48,1664]{1,0:T(8,128)(2,1)S(1)}, u32[]{:S(2)}, u32[]{:S(2)}) collective-permute-start(bf16[48,1664]{1,0:T(8,128)(2,1)S(1)} %get-tuple-element.46), channel_id=1, source_target_pairs={{0,4},{1,13},{2,6},{3,15},{4,0},{5,9},{6,2},{7,11},{8,12},{9,5},{1... | collective-permute-start | bytes 479240 | tf_op jit(solution)/shard_map/ppermute | solution.py:32
  105.4 14.4 %collective-permute-start.22 = (bf16[48,1664]{1,0:T(8,128)(2,1)S(1)}, bf16[48,1664]{1,0:T(8,128)(2,1)S(1)}, u32[]{:S(2)}, u32[]{:S(2)}) collective-permute-start(bf16[48,1664]{1,0:T(8,128)(2,1)S(1)} %get-tuple-element.45), channel_id=1, source_target_pairs={{0,4},{1,13},{2,6},{3,15},{4,0},{5,9},{6,2},{7,11},{8,12},{9,5},{1... | collective-permute-start | bytes 479240 | tf_op jit(solution)/shard_map/ppermute | solution.py:32
  107.9 11.9 %collective-permute-start.21 = (bf16[48,1536]{1,0:T(8,128)(2,1)S(1)}, bf16[48,1536]{1,0:T(8,128)(2,1)S(1)}, u32[]{:S(2)}, u32[]{:S(2)}) collective-permute-start(bf16[48,1536]{1,0:T(8,128)(2,1)S(1)} %add_convert_fusion.1), channel_id=1, source_target_pairs={{0,4},{1,13},{2,6},{3,15},{4,0},{5,9},{6,2},{7,11},{8,12},{9,5},{1... | collective-permute-start | bytes 442376 | tf_op jit(solution)/shard_map/ppermute | solution.py:32
  115.9 9.8 %collective-permute-start.24 = (bf16[48,1664]{1,0:T(8,128)(2,1)S(1)}, bf16[48,1664]{1,0:T(8,128)(2,1)S(1)}, u32[]{:S(2)}, u32[]{:S(2)}) collective-permute-start(bf16[48,1664]{1,0:T(8,128)(2,1)S(1)} %add_convert_fusion), channel_id=1, source_target_pairs={{0,12},{1,5},{2,14},{3,7},{4,8},{5,1},{6,10},{7,3},{8,4},{9,13},{1... | collective-permute-start | bytes 479240 | tf_op jit(solution)/shard_map/ppermute | solution.py:32
